TPU v7x, 32 devices: a whole 2x2x4 slice. The times are simulated.
32 devices in a mesh: row: 4 (over x, core), col: 8 (over z, y).
Axes of the slice: x: 2, y: 2, z: 4, core: 2. Of those that a mesh axis runs over, the one named last changes fastest.
Arguments:
- tokens: bfloat16 [128, 8192], P('col', 'row'), may hold values from -6 to 6
- cotangent: bfloat16 [128, 8192], P('col', 'row'), may hold values from -1.5 to 1.5
- gate_weight: bfloat16 [8192, 14336], P('row', 'col'), may hold values from -0.0625 to 0.0625
- up_weight: bfloat16 [8192, 14336], P('row', 'col'), may hold values from -0.0625 to 0.0625
- down_weight: bfloat16 [14336, 8192], P('col', 'row'), may hold values from -0.046875 to 0.046875
Outputs:
- grad_tokens: bfloat16 [128, 8192], P('col', 'row')
- grad_gate: bfloat16 [8192, 14336], P('row', 'col')
- grad_up: bfloat16 [8192, 14336], P('row', 'col')
- grad_down: bfloat16 [14336, 8192], P('col', 'row')
All inputs are finite; a program needn't handle non-finite values.
Results may differ from a plain program's by a relative error of at most 0.0051.
Values may be sent and summed in bfloat16 or wider, within the bound.
A program may use at most 128 MiB of HBM per device.

v0:
```python
import jax
import jax.numpy as jnp
from jax import lax
from jax.sharding import PartitionSpec as P


def contract_last(left, right):
    return lax.dot_general(
        left, right, (((1,), (1,)), ((), ())), preferred_element_type=jnp.float32
    )


def contract_first(left, right):
    return lax.dot_general(
        left, right, (((0,), (0,)), ((), ())), preferred_element_type=jnp.float32
    )


def gating(gate, up, grad_hidden):
    sig = jax.nn.sigmoid(gate)
    act = gate * sig
    hidden = (act * up).astype(jnp.bfloat16)
    d_up = (grad_hidden * act).astype(jnp.bfloat16)
    d_gate = (grad_hidden * up * sig * (1.0 + gate * (1.0 - sig))).astype(jnp.bfloat16)
    return (jnp.concatenate([d_gate, d_up], axis=1), hidden)


def local(tokens, cotangent, gate_weight, up_weight, down_weight):
    tok_all, cot_all = (
        lax.all_gather(tokens, "col", axis=0, tiled=True),
        lax.all_gather(cotangent, "col", axis=0, tiled=True),
    )
    width = gate_weight.shape[1]
    both_weights = jnp.concatenate([gate_weight, up_weight], axis=1)
    piece = tok_all
    summed = lax.psum_scatter(
        jnp.dot(piece, both_weights, preferred_element_type=jnp.float32),
        "row",
        scatter_dimension=0,
        tiled=True,
    )
    piece = cot_all
    grad_hidden = lax.psum_scatter(
        contract_last(piece, down_weight), "row", scatter_dimension=0, tiled=True
    )
    paired, hidden = gating(summed[:, :width], summed[:, width:], grad_hidden)
    paired_all, hidden_all = (
        lax.all_gather(paired, "row", axis=0, tiled=True),
        lax.all_gather(hidden, "row", axis=0, tiled=True),
    )
    grad_both = contract_first(tok_all, paired_all)
    grad_gate = grad_both[:, :width].astype(jnp.bfloat16)
    grad_up = grad_both[:, width:].astype(jnp.bfloat16)
    grad_down = contract_first(hidden_all, cot_all).astype(jnp.bfloat16)
    piece = paired_all
    grad_tokens = lax.psum_scatter(
        contract_last(piece, both_weights), "col", scatter_dimension=0, tiled=True
    ).astype(jnp.bfloat16)
    return (grad_tokens, grad_gate, grad_up, grad_down)


def solution(mesh):
    return jax.shard_map(
        local,
        mesh=mesh,
        in_specs=(
            P("col", "row"),
            P("col", "row"),
            P("row", "col"),
            P("row", "col"),
            P("col", "row"),
        ),
        out_specs=(P("col", "row"), P("row", "col"), P("row", "col"), P("col", "row")),
        check_vma=False,
    )
```

profile of v0, /device:TPU:0, one launch (start us, length us, event | category | flops | bytes accessed | tf_op | source)
XLA Modules:
  0.0 231.6 jit_solution(5471020805838805017)
XLA Ops:
  7.2 0.0 reduce-scatter.4.cloned.1.call-start
  7.2 33.2 %all_gather.12 = bf16[128,2048]{1,0:T(8,128)(2,1)S(1)} all-gather(bf16[16,2048]{1,0:T(8,128)(2,1)} %param.6), channel_id=1, replica_groups=mesh['row'=4,'col'=8] {'col'}, dimensions={0}, use_global_device_ids=true | all-gather | bytes 589824 | tf_op jit(solution)/shard_map/all_gather | solution.py:31
  40.4 6.5 %fusion.3 = f32[128,1792]{1,0:T(8,128)} fusion(bf16[128,2048]{1,0:T(8,128)(2,1)S(1)} %all_gather.12, bf16[1792,2048]{1,0:T(8,128)(2,1)} %param.9), kind=kOutput, calls=%fused_computation.13 | convolution fusion | flops 939524096 | bytes 8781824 | tf_op jit(solution)/shard_map/dot_general | solution.py:8
  47.0 0.0 reduce-scatter.4.cloned.1.call-update
  47.0 0.0 copy-start
  47.0 0.0 reduce-scatter.6.cloned.1.call-start
  47.1 6.6 %constant_dynamic-update-slice_fusion.1 = bf16[2048,3584]{1,0:T(8,128)(2,1)} fusion(bf16[2048,1792]{1,0:T(8,128)(2,1)} %param.7), kind=kLoop, calls=%fused_computation.11 | loop fusion | bytes 14680064
  53.7 0.0 copy-done
  53.7 31.3 %all_gather.13 = bf16[128,2048]{1,0:T(8,128)(2,1)S(1)} all-gather(bf16[16,2048]{1,0:T(8,128)(2,1)S(1)} %copy-done), channel_id=1, replica_groups=mesh['row'=4,'col'=8] {'col'}, dimensions={0}, use_global_device_ids=true | all-gather | bytes 589824 | tf_op jit(solution)/shard_map/all_gather | solution.py:30
  84.9 6.6 %constant_dynamic-update-slice_fusion = bf16[2048,3584]{1,0:T(8,128)(2,1)} fusion(bf16[2048,3584]{1,0:T(8,128)(2,1)} %constant_dynamic-update-slice_fusion.1, bf16[2048,1792]{1,0:T(8,128)(2,1)} %param.8), kind=kLoop, calls=%fused_computation.10 | loop fusion | bytes 14680064 | tf_op jit(solution)/shard_map/concatenate | solution.py:34
  91.5 8.5 %convolution_bitcast_fusion = f32[128,3584]{1,0:T(8,128)} fusion(bf16[128,2048]{1,0:T(8,128)(2,1)S(1)} %all_gather.13, bf16[2048,3584]{1,0:T(8,128)(2,1)} %constant_dynamic-update-slice_fusion), kind=kOutput, calls=%fused_computation.3 | convolution fusion | flops 1879048192 | bytes 17039360 | tf_op jit(solution)/shard_map/dot_general | solution.py:37
  100.0 0.0 reduce-scatter.6.cloned.1.call-update
  100.0 0.0 reduce-scatter.8.cloned.1.call-start
  100.1 0.0 reduce-scatter.4.cloned.1.call-done
  100.1 31.1 %reduce-scatter.6.cloned.1.call-done = f32[32,3584]{1,0:T(8,128)} async-done(((f32[128,3584]{1,0:T(8,128)}), f32[32,3584]{1,0:T(8,128)}) %reduce-scatter.6.cloned.1.call-update) | async-done | bytes 458768 | tf_op jit(solution)/shard_map/reduce_scatter | solution.py:36
  131.2 1.3 multiply_convert_fusion.2
  132.5 8.9 %all_gather.14 = bf16[128,3584]{1,0:T(8,128)(2,1)S(1)} all-gather(bf16[32,3584]{1,0:T(8,128)(2,1)S(1)} %pad_maximum_fusion), channel_id=1, replica_groups=mesh['row'=4,'col'=8] {'row'}, dimensions={0}, use_global_device_ids=true | all-gather | bytes 1146880 | tf_op jit(solution)/shard_map/all_gather | solution.py:48
  141.4 10.9 %fusion.4 = f32[128,2048]{1,0:T(8,128)} fusion(bf16[128,3584]{1,0:T(8,128)(2,1)S(1)} %all_gather.14, bf16[2048,3584]{1,0:T(8,128)(2,1)} %constant_dynamic-update-slice_fusion), kind=kOutput, calls=%fused_computation.14 | convolution fusion | flops 1879048192 | bytes 16646144 | tf_op jit(solution)/shard_map/dot_general | solution.py:8
  152.3 7.3 %fusion = bf16[2048,3584]{0,1:T(8,128)(2,1)} fusion(bf16[128,3584]{1,0:T(8,128)(2,1)S(1)} %all_gather.14, bf16[128,2048]{1,0:T(8,128)(2,1)S(1)} %all_gather.13), kind=kOutput, calls=%fused_computation.1 | convolution fusion | flops 1886388224 | bytes 16121856 | tf_op jit(solution)/shard_map/dot_general | solution.py:14
  159.6 0.0 reduce-scatter.8.cloned.1.call-update
  159.6 10.8 %fusion.2 = (bf16[2048,1792]{0,1:T(8,128)(2,1)}, bf16[2048,1792]{0,1:T(8,128)(2,1)}) fusion(bf16[2048,3584]{0,1:T(8,128)(2,1)} %fusion), kind=kLoop, calls=%fused_computation.12 | loop fusion | bytes 29360128 | tf_op jit(solution)/shard_map/slice | solution.py:53
  170.5 10.0 %copy.10 = bf16[2048,1792]{1,0:T(8,128)(2,1)} copy(bf16[2048,1792]{0,1:T(8,128)(2,1)} %get-tuple-element.9) | data formatting | bytes 14680064
  180.4 9.9 %copy.11 = bf16[2048,1792]{1,0:T(8,128)(2,1)} copy(bf16[2048,1792]{0,1:T(8,128)(2,1)} %get-tuple-element.8) | data formatting | bytes 14680064
  190.4 7.0 %all_gather.15 = bf16[128,1792]{1,0:T(8,128)(2,1)S(1)} all-gather(bf16[32,1792]{1,0:T(8,128)(2,1)S(1)} %get-tuple-element.12), channel_id=1, replica_groups=mesh['row'=4,'col'=8] {'row'}, dimensions={0}, use_global_device_ids=true | all-gather | bytes 573440 | tf_op jit(solution)/shard_map/all_gather | solution.py:49
  197.4 5.1 %convolution_convert_fusion.1 = bf16[1792,2048]{1,0:T(8,128)(2,1)} fusion(bf16[128,1792]{1,0:T(8,128)(2,1)S(1)} %all_gather.15, bf16[128,2048]{1,0:T(8,128)(2,1)S(1)} %all_gather.12), kind=kOutput, calls=%fused_computation.2 | convolution fusion | flops 943194112 | bytes 8323072 | tf_op jit(solution)/shard_map/dot_general | solution.py:14
  202.5 21.0 %reduce-scatter.8.cloned.1.call-done = f32[16,2048]{1,0:T(8,128)} async-done(((f32[128,2048]{1,0:T(8,128)}), f32[16,2048]{1,0:T(8,128)}) %reduce-scatter.8.cloned.1.call-update) | async-done | bytes 131088 | tf_op jit(solution)/shard_map/reduce_scatter | solution.py:56
  223.5 1.5 convert_element_type.19
  (1 shorter events, 0.0 us)
Async XLA Ops:
  7.2 92.9 %reduce-scatter.4.cloned.1.call-start = ((), (), s32[]{:S(2)}) async-start(), calls=%async_computation.3 | async-start | bytes 1146880 | tf_op jit(solution)/shard_map/reduce_scatter | solution.py:43
  47.0 6.7 %copy-start = (bf16[16,2048]{1,0:T(8,128)(2,1)S(1)}, bf16[16,2048]{1,0:T(8,128)(2,1)}, u32[]{:S(2)}) copy-start(bf16[16,2048]{1,0:T(8,128)(2,1)} %param.5) | copy-start | bytes 196612
  47.0 84.2 %reduce-scatter.6.cloned.1.call-start = ((), (), s32[]{:S(2)}) async-start(), calls=%async_computation.4 | async-start | bytes 2293760 | tf_op jit(solution)/shard_map/reduce_scatter | solution.py:36
  100.0 123.5 %reduce-scatter.8.cloned.1.call-start = ((), (), s32[]{:S(2)}) async-start(), calls=%async_computation.5 | async-start | bytes 1179648 | tf_op jit(solution)/shard_map/reduce_scatter | solution.py:56
Sparse Core Ops, SparseCore 0:
  47.1 25.1 reduce-scatter.3
  100.1 30.9 reduce-scatter.5
  159.7 63.7 reduce-scatter.7
where the time goes:
time: 232 us
  blocking collectives  80.4 us (35%)
  waiting for transfers between devices  52.1 us (22%)
  local copies, waits for them, and re-layouts  43.9 us (19%)
  matrix products  38.4 us (17%)
  between operations  13.8 us (6%)
  other arithmetic  2.84 us (1%)
    all_gather x1, blocking collectives, local(): lax.all_gather(cotangent, 'col', axis=0, tiled=True)  33.2 us
    all_gather x1, blocking collectives, local(): lax.all_gather(tokens, 'col', axis=0, tiled=True)  31.3 us
    reduce_scatter x1, waiting for transfers between devices, local(): lax.psum_scatter(jnp.dot(piece, both_weights, preferred_element_type=jnp....  31.1 us
    unnamed x5, local copies, waits for them, and re-layouts  26.5 us
    reduce_scatter x1, waiting for transfers between devices, local(): lax.psum_scatter(contract_last(piece, both_weights), 'col', scatter_dimen...  21 us
    dot_general x2, matrix products, contract_last(): lax.dot_general(left, right, (((1,), (1,)), ((), ())), preferred_element_...  17.4 us
    dot_general x2, matrix products, contract_first(): lax.dot_general(left, right, (((0,), (0,)), ((), ())), preferred_element_...  12.4 us
    slice x1, local copies, waits for them, and re-layouts, local(): grad_up = grad_both[:, width:].astype(jnp.bfloat16)  10.8 us
  transfers between devices with their start and end apart: 3, of which 2 were waited for; matrix products, arithmetic and copies ran while one was open for 25% of the time, Pallas kernels for 0%

commit v1 on v0

--- a/solution.py
+++ b/solution.py
@@ -2,6 +2,27 @@
 import jax.numpy as jnp
 from jax import lax
 from jax.sharding import PartitionSpec as P
+
+
+def gather_around(array, axis, dim):
+    size, mine, width = (lax.axis_size(axis), lax.axis_index(axis), array.shape[dim])
+    right = [(i, (i + 1) % size) for i in range(size)]
+    left = [(i, (i - 1) % size) for i in range(size)]
+    result = jnp.zeros((*array.shape[:dim], size * width, *array.shape[dim + 1 :]), array.dtype)
+    result = lax.dynamic_update_slice_in_dim(result, array, mine * width, axis=dim)
+    from_left = from_right = array
+    halfway = size // 2
+    for step in range(1, halfway + 1):
+        from_left = lax.ppermute(from_left, axis, right)
+        result = lax.dynamic_update_slice_in_dim(
+            result, from_left, (mine - step) % size * width, axis=dim
+        )
+        if step < size - halfway:
+            from_right = lax.ppermute(from_right, axis, left)
+            result = lax.dynamic_update_slice_in_dim(
+                result, from_right, (mine + step) % size * width, axis=dim
+            )
+    return result
 
 
 def contract_last(left, right):
@@ -27,7 +48,7 @@
 
 def local(tokens, cotangent, gate_weight, up_weight, down_weight):
     tok_all, cot_all = (
-        lax.all_gather(tokens, "col", axis=0, tiled=True),
+        gather_around(tokens, "col", 0),
         lax.all_gather(cotangent, "col", axis=0, tiled=True),
     )
     width = gate_weight.shape[1]

time: 232 us -> 223 us (0.961)
  blocking collectives: 80.4 us -> 47.5 us
  waiting for transfers between devices: 52.1 us -> 79.9 us
  local copies, waits for them, and re-layouts: 43.9 us -> 23.8 us
  starting transfers between devices: 0.12 us -> 15.7 us
    all_gather x1 -> x0, blocking collectives: 31.3 us -> none  [local(): lax.all_gather(tokens, 'col', axis=0, tiled=True)]
    reduce_scatter x1, waiting for transfers between devices: 21 us -> 41.1 us  [local(): lax.psum_scatter(contract_last(piece, both_weights), 'col', scatter_dimen...]
    unnamed x5 -> x3, local copies, waits for them, and re-layouts: 26.5 us -> 6.64 us
    ppermute x0 -> x7, starting transfers between devices: none -> 15.6 us  [the longest x3 12.5 us: gather_around(): from_right = lax.ppermute(from_right, axis, left)]
    ppermute x0 -> x7, waiting for transfers between devices: none -> 11.3 us  [the longest x4 11.3 us: gather_around(): from_left = lax.ppermute(from_left, axis, right)]
    reduce_scatter x1, waiting for transfers between devices: 31.1 us -> 27.3 us  [local(): lax.psum_scatter(jnp.dot(piece, both_weights, preferred_element_type=jnp....]
  transfers between devices with their start and end apart: 3 -> 10, of which waited for: 2 -> 5; matrix products, arithmetic and copies ran while one was open for 25% -> 20% of each run, Pallas kernels for 0% -> 0%
where the time goes in v1:
time: 223 us; the launch traced here: 222 us
  waiting for transfers between devices  79.9 us (36%)
  blocking collectives  47.5 us (21%)
  matrix products  38.4 us (17%)
  local copies, waits for them, and re-layouts  23.8 us (11%)
  starting transfers between devices  15.7 us (7%)
  between operations  14 us (6%)
  other arithmetic  2.84 us (1%)
    reduce_scatter x1, waiting for transfers between devices, local(): lax.psum_scatter(contract_last(piece, both_weights), 'col', scatter_dimen...  41.1 us
    all_gather x1, blocking collectives, local(): lax.all_gather(cotangent, 'col', axis=0, tiled=True)  31.5 us
    reduce_scatter x1, waiting for transfers between devices, local(): lax.psum_scatter(jnp.dot(piece, both_weights, preferred_element_type=jnp....  27.3 us
    dot_general x2, matrix products, contract_last(): lax.dot_general(left, right, (((1,), (1,)), ((), ())), preferred_element_...  17.4 us
    ppermute x3, starting transfers between devices, gather_around(): from_right = lax.ppermute(from_right, axis, left)  12.5 us
    dot_general x2, matrix products, contract_first(): lax.dot_general(left, right, (((0,), (0,)), ((), ())), preferred_element_...  12.5 us
    ppermute x4, waiting for transfers between devices, gather_around(): from_left = lax.ppermute(from_left, axis, right)  11.3 us
    slice x1, local copies, waits for them, and re-layouts, local(): grad_up = grad_both[:, width:].astype(jnp.bfloat16)  10.5 us
  transfers between devices with their start and end apart: 10, of which 5 were waited for; matrix products, arithmetic and copies ran while one was open for 20% of the time, Pallas kernels for 0%

profile of v1, /device:TPU:0, one launch (start us, length us, event | category | flops | bytes accessed | tf_op | source)
XLA Modules:
  0.0 222.2 jit_solution(15179109896858008889)
XLA Ops:
  7.2 0.0 reduce-scatter.4.cloned.1.call-start
  7.2 3.0 %collective-permute-start = (bf16[16,2048]{1,0:T(8,128)(2,1)}, bf16[16,2048]{1,0:T(8,128)(2,1)S(1)}, u32[]{:S(2)}, u32[]{:S(2)}) collective-permute-start(bf16[16,2048]{1,0:T(8,128)(2,1)} %param.5), channel_id=1, source_target_pairs={{0,1},{1,2},{2,3},{3,4},{4,5},{5,6},{6,7},{7,0},{8,9},{9,10},{10,1... | collective-permute-start | bytes 196616 | tf_op jit(solution)/shard_map/ppermute | solution.py:16
  10.2 3.1 %collective-permute-start.1 = (bf16[16,2048]{1,0:T(8,128)(2,1)}, bf16[16,2048]{1,0:T(8,128)(2,1)S(1)}, u32[]{:S(2)}, u32[]{:S(2)}) collective-permute-start(bf16[16,2048]{1,0:T(8,128)(2,1)} %param.5), channel_id=1, source_target_pairs={{0,7},{1,0},{2,1},{3,2},{4,3},{5,4},{6,5},{7,6},{8,15},{9,8},{10,9... | collective-permute-start | bytes 196616 | tf_op jit(solution)/shard_map/ppermute | solution.py:21
  13.3 31.5 %all_gather.9 = bf16[128,2048]{1,0:T(8,128)(2,1)S(1)} all-gather(bf16[16,2048]{1,0:T(8,128)(2,1)} %param.6), channel_id=1, replica_groups=mesh['row'=4,'col'=8] {'col'}, dimensions={0}, use_global_device_ids=true | all-gather | bytes 589824 | tf_op jit(solution)/shard_map/all_gather | solution.py:52
  44.8 6.6 %fusion.2 = f32[128,1792]{1,0:T(8,128)} fusion(bf16[128,2048]{1,0:T(8,128)(2,1)S(1)} %all_gather.9, bf16[1792,2048]{1,0:T(8,128)(2,1)} %param.9), kind=kOutput, calls=%fused_computation.19 | convolution fusion | flops 939524096 | bytes 8781824 | tf_op jit(solution)/shard_map/dot_general | solution.py:29
  51.4 0.0 reduce-scatter.4.cloned.1.call-update
  51.4 0.0 reduce-scatter.6.cloned.1.call-start
  51.5 0.0 copy-start
  51.5 6.6 %constant_dynamic-update-slice_fusion.1 = bf16[2048,3584]{1,0:T(8,128)(2,1)} fusion(bf16[2048,1792]{1,0:T(8,128)(2,1)} %param.7), kind=kLoop, calls=%fused_computation.9 | loop fusion | bytes 14680064
  58.1 6.6 %constant_dynamic-update-slice_fusion = bf16[2048,3584]{1,0:T(8,128)(2,1)} fusion(bf16[2048,3584]{1,0:T(8,128)(2,1)} %constant_dynamic-update-slice_fusion.1, bf16[2048,1792]{1,0:T(8,128)(2,1)} %param.8), kind=kLoop, calls=%fused_computation.8 | loop fusion | bytes 14680064 | tf_op jit(solution)/shard_map/concatenate | solution.py:55
  64.9 0.0 collective-permute-done
  65.0 0.1 collective-permute-start.2
  65.0 4.7 %collective-permute-start.3 = (bf16[16,2048]{1,0:T(8,128)(2,1)S(1)}, bf16[16,2048]{1,0:T(8,128)(2,1)S(1)}, u32[]{:S(2)}, u32[]{:S(2)}) collective-permute-start(bf16[16,2048]{1,0:T(8,128)(2,1)S(1)} %collective-permute-done.1), channel_id=1, source_target_pairs={{0,7},{1,0},{2,1},{3,2},{4,3},{5,4},{6,5},{7,6},{8,15},{9,8},{10,9... | collective-permute-start | bytes 196616 | tf_op jit(solution)/shard_map/ppermute | solution.py:21
  69.8 2.2 collective-permute-done.2
  72.0 4.7 %collective-permute-start.5 = (bf16[16,2048]{1,0:T(8,128)(2,1)S(1)}, bf16[16,2048]{1,0:T(8,128)(2,1)S(1)}, u32[]{:S(2)}, u32[]{:S(2)}) collective-permute-start(bf16[16,2048]{1,0:T(8,128)(2,1)S(1)} %collective-permute-done.3), channel_id=1, source_target_pairs={{0,7},{1,0},{2,1},{3,2},{4,3},{5,4},{6,5},{7,6},{8,15},{9,8},{10,9... | collective-permute-start | bytes 196616 | tf_op jit(solution)/shard_map/ppermute | solution.py:21
  76.7 2.2 collective-permute-done.4
  79.0 6.9 %collective-permute-done.6 = bf16[16,2048]{1,0:T(8,128)(2,1)S(1)} collective-permute-done((bf16[16,2048]{1,0:T(8,128)(2,1)S(1)}, bf16[16,2048]{1,0:T(8,128)(2,1)S(1)}, u32[]{:S(2)}, u32[]{:S(2)}) %collective-permute-start.6) | collective-permute-done | bytes 65568 | tf_op jit(solution)/shard_map/ppermute | solution.py:16
  85.9 8.5 %fusion.3 = f32[128,3584]{1,0:T(8,128)} fusion(bf16[128,2048]{1,0:T(8,128)(2,1)S(1)} %constant_dynamic-update-slice_fusion.2, bf16[2048,3584]{1,0:T(8,128)(2,1)} %constant_dynamic-update-slice_fusion), kind=kOutput, calls=%fused_computation.20 | convolution fusion | flops 1879048192 | bytes 17039360 | tf_op jit(solution)/shard_map/dot_general | solution.py:58
  94.4 0.0 reduce-scatter.6.cloned.1.call-update
  94.4 0.0 reduce-scatter.8.cloned.1.call-start
  94.5 0.0 reduce-scatter.4.cloned.1.call-done
  94.5 27.3 %reduce-scatter.6.cloned.1.call-done = f32[32,3584]{1,0:T(8,128)} async-done(((f32[128,3584]{1,0:T(8,128)}), f32[32,3584]{1,0:T(8,128)}) %reduce-scatter.6.cloned.1.call-update) | async-done | bytes 458768 | tf_op jit(solution)/shard_map/reduce_scatter | solution.py:57
  121.8 1.3 multiply_convert_fusion.2
  123.1 8.9 %all_gather.10 = bf16[128,3584]{1,0:T(8,128)(2,1)S(1)} all-gather(bf16[32,3584]{1,0:T(8,128)(2,1)S(1)} %pad_maximum_fusion), channel_id=1, replica_groups=mesh['row'=4,'col'=8] {'row'}, dimensions={0}, use_global_device_ids=true | all-gather | bytes 1146880 | tf_op jit(solution)/shard_map/all_gather | solution.py:69
  132.0 10.9 %fusion.4 = f32[128,2048]{1,0:T(8,128)} fusion(bf16[128,3584]{1,0:T(8,128)(2,1)S(1)} %all_gather.10, bf16[2048,3584]{1,0:T(8,128)(2,1)} %constant_dynamic-update-slice_fusion), kind=kOutput, calls=%fused_computation.21 | convolution fusion | flops 1879048192 | bytes 16646144 | tf_op jit(solution)/shard_map/dot_general | solution.py:29
  142.9 7.3 %convolution_convert_fusion = bf16[2048,3584]{1,0:T(8,128)(2,1)} fusion(bf16[128,2048]{1,0:T(8,128)(2,1)S(1)} %constant_dynamic-update-slice_fusion.2, bf16[128,3584]{1,0:T(8,128)(2,1)S(1)} %all_gather.10), kind=kOutput, calls=%fused_computation | convolution fusion | flops 1886388224 | bytes 16121856 | tf_op jit(solution)/shard_map/dot_general | solution.py:35
  150.2 0.0 reduce-scatter.8.cloned.1.call-update
  150.2 7.1 %all_gather.11 = bf16[128,1792]{1,0:T(8,128)(2,1)S(1)} all-gather(bf16[32,1792]{1,0:T(8,128)(2,1)S(1)} %get-tuple-element.8), channel_id=1, replica_groups=mesh['row'=4,'col'=8] {'row'}, dimensions={0}, use_global_device_ids=true | all-gather | bytes 573440 | tf_op jit(solution)/shard_map/all_gather | solution.py:70
  157.4 5.1 %convolution_convert_fusion.1 = bf16[1792,2048]{1,0:T(8,128)(2,1)} fusion(bf16[128,1792]{1,0:T(8,128)(2,1)S(1)} %all_gather.11, bf16[128,2048]{1,0:T(8,128)(2,1)S(1)} %all_gather.9), kind=kOutput, calls=%fused_computation.1 | convolution fusion | flops 943194112 | bytes 8323072 | tf_op jit(solution)/shard_map/dot_general | solution.py:35
  162.5 10.5 %fusion.1 = (bf16[2048,1792]{1,0:T(8,128)(2,1)}, bf16[2048,1792]{1,0:T(8,128)(2,1)}) fusion(bf16[2048,3584]{1,0:T(8,128)(2,1)} %convolution_convert_fusion), kind=kLoop, calls=%fused_computation.18 | loop fusion | bytes 29360128 | tf_op jit(solution)/shard_map/slice | solution.py:74
  173.0 41.1 %reduce-scatter.8.cloned.1.call-done = f32[16,2048]{1,0:T(8,128)} async-done(((f32[128,2048]{1,0:T(8,128)}), f32[16,2048]{1,0:T(8,128)}) %reduce-scatter.8.cloned.1.call-update) | async-done | bytes 131088 | tf_op jit(solution)/shard_map/reduce_scatter | solution.py:77
  214.1 1.5 convert_element_type.19
  (16 shorter events, 0.2 us)
Async XLA Ops:
  7.2 87.3 %reduce-scatter.4.cloned.1.call-start = ((), (), s32[]{:S(2)}) async-start(), calls=%async_computation.3 | async-start | bytes 1146880 | tf_op jit(solution)/shard_map/reduce_scatter | solution.py:64
  7.2 57.7 %collective-permute-start = (bf16[16,2048]{1,0:T(8,128)(2,1)}, bf16[16,2048]{1,0:T(8,128)(2,1)S(1)}, u32[]{:S(2)}, u32[]{:S(2)}) collective-permute-start(bf16[16,2048]{1,0:T(8,128)(2,1)} %param.5), channel_id=1, source_target_pairs={{0,1},{1,2},{2,3},{3,4},{4,5},{5,6},{6,7},{7,0},{8,9},{9,10},{10,1... | collective-permute-start | bytes 196616 | tf_op jit(solution)/shard_map/ppermute | solution.py:16
  10.2 54.8 %collective-permute-start.1 = (bf16[16,2048]{1,0:T(8,128)(2,1)}, bf16[16,2048]{1,0:T(8,128)(2,1)S(1)}, u32[]{:S(2)}, u32[]{:S(2)}) collective-permute-start(bf16[16,2048]{1,0:T(8,128)(2,1)} %param.5), channel_id=1, source_target_pairs={{0,7},{1,0},{2,1},{3,2},{4,3},{5,4},{6,5},{7,6},{8,15},{9,8},{10,9... | collective-permute-start | bytes 196616 | tf_op jit(solution)/shard_map/ppermute | solution.py:21
  51.4 70.4 %reduce-scatter.6.cloned.1.call-start = ((), (), s32[]{:S(2)}) async-start(), calls=%async_computation.4 | async-start | bytes 2293760 | tf_op jit(solution)/shard_map/reduce_scatter | solution.py:57
  51.5 13.3 %copy-start = (bf16[16,2048]{1,0:T(8,128)(2,1)S(1)}, bf16[16,2048]{1,0:T(8,128)(2,1)}, u32[]{:S(2)}) copy-start(bf16[16,2048]{1,0:T(8,128)(2,1)} %param.5) | copy-start | bytes 196612
  65.0 7.0 %collective-permute-start.2 = (bf16[16,2048]{1,0:T(8,128)(2,1)S(1)}, bf16[16,2048]{1,0:T(8,128)(2,1)S(1)}, u32[]{:S(2)}, u32[]{:S(2)}) collective-permute-start(bf16[16,2048]{1,0:T(8,128)(2,1)S(1)} %collective-permute-done), channel_id=1, source_target_pairs={{0,1},{1,2},{2,3},{3,4},{4,5},{5,6},{6,7},{7,0},{8,9},{9,10},{10,1... | collective-permute-start | bytes 196616 | tf_op jit(solution)/shard_map/ppermute | solution.py:16
  65.0 6.9 %collective-permute-start.3 = (bf16[16,2048]{1,0:T(8,128)(2,1)S(1)}, bf16[16,2048]{1,0:T(8,128)(2,1)S(1)}, u32[]{:S(2)}, u32[]{:S(2)}) collective-permute-start(bf16[16,2048]{1,0:T(8,128)(2,1)S(1)} %collective-permute-done.1), channel_id=1, source_target_pairs={{0,7},{1,0},{2,1},{3,2},{4,3},{5,4},{6,5},{7,6},{8,15},{9,8},{10,9... | collective-permute-start | bytes 196616 | tf_op jit(solution)/shard_map/ppermute | solution.py:21
  72.0 7.0 %collective-permute-start.4 = (bf16[16,2048]{1,0:T(8,128)(2,1)S(1)}, bf16[16,2048]{1,0:T(8,128)(2,1)S(1)}, u32[]{:S(2)}, u32[]{:S(2)}) collective-permute-start(bf16[16,2048]{1,0:T(8,128)(2,1)S(1)} %collective-permute-done.2), channel_id=1, source_target_pairs={{0,1},{1,2},{2,3},{3,4},{4,5},{5,6},{6,7},{7,0},{8,9},{9,10},{10,1... | collective-permute-start | bytes 196616 | tf_op jit(solution)/shard_map/ppermute | solution.py:16
  72.0 7.0 %collective-permute-start.5 = (bf16[16,2048]{1,0:T(8,128)(2,1)S(1)}, bf16[16,2048]{1,0:T(8,128)(2,1)S(1)}, u32[]{:S(2)}, u32[]{:S(2)}) collective-permute-start(bf16[16,2048]{1,0:T(8,128)(2,1)S(1)} %collective-permute-done.3), channel_id=1, source_target_pairs={{0,7},{1,0},{2,1},{3,2},{4,3},{5,4},{6,5},{7,6},{8,15},{9,8},{10,9... | collective-permute-start | bytes 196616 | tf_op jit(solution)/shard_map/ppermute | solution.py:21
  78.9 7.0 %collective-permute-start.6 = (bf16[16,2048]{1,0:T(8,128)(2,1)S(1)}, bf16[16,2048]{1,0:T(8,128)(2,1)S(1)}, u32[]{:S(2)}, u32[]{:S(2)}) collective-permute-start(bf16[16,2048]{1,0:T(8,128)(2,1)S(1)} %collective-permute-done.4), channel_id=1, source_target_pairs={{0,1},{1,2},{2,3},{3,4},{4,5},{5,6},{6,7},{7,0},{8,9},{9,10},{10,1... | collective-permute-start | bytes 196616 | tf_op jit(solution)/shard_map/ppermute | solution.py:16
  94.4 119.7 %reduce-scatter.8.cloned.1.call-start = ((), (), s32[]{:S(2)}) async-start(), calls=%async_computation.5 | async-start | bytes 1179648 | tf_op jit(solution)/shard_map/reduce_scatter | solution.py:77
Sparse Core Ops, SparseCore 0:
  51.5 22.7 reduce-scatter.3
  94.5 27.2 reduce-scatter.5
  150.4 63.7 reduce-scatter.7
